TPU v7x, 256 devices: a whole 4x4x8 slice. The times are simulated.
256 devices in a mesh: batch: 8 (over y, x_lo), tm: 32 (over x_hi, z, core).
Axes of the slice: x: 4 (x_hi: 2, x_lo: 2; x = x_hi * 2 + x_lo), y: 4, z: 8, core: 2. Of those that a mesh axis runs over, the one named last changes fastest.
Arguments:
- inputs: bfloat16 [8, 4096, 1536], P('batch', 'tm'), may hold values from -6 to 6
- lengths: int32 [8], P('batch'), may hold values from 2048 to 4096, as said below
- kernel: float32 [31, 1536], replicated, may hold values from -1 to 1
- norm_gain: float32 [1536], replicated, may hold values from 0.25 to 1.75
- weight: bfloat16 [1536, 1536], P('batch'), may hold values from -0.15625 to 0.15625
- cotangent: bfloat16 [8, 4096, 1536], P('batch', 'tm'), may hold values from -6 to 6
Outputs:
- projected: bfloat16 [8, 4096, 1536], P('batch', 'tm')
- grad_input: bfloat16 [8, 4096, 1536], P('batch', 'tm')
- grad_weight: float32 [1536, 1536], P(('batch', 'tm'))
- grad_kernel: float32 [31, 1536], replicated
- grad_gain: float32 [1536], replicated
Inputs may be any that keep to these rules, and one draw needn't show every extreme that they name: `lengths`: some utterance is valid over all 4096 frames.
All inputs are finite; a program needn't handle non-finite values.
Results may differ from a plain program's by a relative error of at most 0.0049.
Values may be sent and summed in bfloat16 or wider, within the bound.
A program may use at most 64 MiB of HBM per device.

v0:
```python
import jax
import jax.numpy as jnp
from jax import lax
from jax.sharding import PartitionSpec as P


def padded_2(cells, sides, width):
    for axis, dim in sides:
        count = lax.axis_size(axis)
        ends = count - 1
        head = lax.slice_in_dim(cells, 0, width, axis=dim)
        tail = lax.slice_in_dim(cells, cells.shape[dim] - width, cells.shape[dim], axis=dim)
        cells = jnp.concatenate(
            [
                lax.ppermute(tail, axis, [(i, (i + 1) % count) for i in range(ends)]),
                cells,
                lax.ppermute(head, axis, [((i + 1) % count, i) for i in range(ends)]),
            ],
            axis=dim,
        )
    return cells


def conv_taps(padded, kernel, frames):
    total = jnp.zeros((padded.shape[0], frames, padded.shape[2]), jnp.float32)
    for tap in range(kernel.shape[0]):
        total = total + kernel[tap] * padded[:, tap : tap + frames, :]
    return total


def norm_forward(convolved):
    average = jnp.mean(convolved, axis=-1, keepdims=True)
    centred = convolved - average
    variance = jnp.mean(centred * centred, axis=-1, keepdims=True)
    inv_scale = lax.rsqrt(variance + 1e-05)
    return (centred * inv_scale, inv_scale)


def norm_backward(act_grad, scaled, normed, inv_scale, norm_gain, live_mask):
    sigmoid_u = jax.nn.sigmoid(scaled)
    scaled_grad = act_grad * sigmoid_u * (1.0 + scaled * (1.0 - sigmoid_u))
    gain_grad = jnp.sum(scaled_grad * normed, axis=(0, 1))
    normed_grad = scaled_grad * norm_gain
    first = jnp.mean(normed_grad, axis=-1, keepdims=True)
    second = jnp.mean(normed_grad * normed, axis=-1, keepdims=True)
    conv_grad = inv_scale * (normed_grad - first - normed * second) * live_mask
    return (gain_grad, conv_grad)


def transposed(left, right):
    return lax.dot_general(
        left, right, (((1,), (1,)), ((), ())), preferred_element_type=jnp.float32
    )


def row_product(columns, grad_rows):
    return lax.dot_general(
        columns, grad_rows, (((0,), (0,)), ((), ())), preferred_element_type=jnp.float32
    )


def on_device(inputs, lengths, kernel, norm_gain, weight, cotangent):
    utterances, frames, features = inputs.shape
    taps = kernel.shape[0]
    reach = (taps - 1) // 2
    position = lax.axis_index("tm") * frames + jnp.arange(frames, dtype=jnp.int32)
    live_mask = (position[None, :] < lengths[:, None]).astype(jnp.float32)[:, :, None]
    masked = inputs * live_mask.astype(jnp.bfloat16)
    padded = padded_2(masked, (("tm", 1),), reach).astype(jnp.float32)
    convolved = conv_taps(padded, kernel, frames) * live_mask
    normed, inv_scale = norm_forward(convolved)
    scaled = normed * norm_gain
    activated = (scaled * jax.nn.sigmoid(scaled)).astype(jnp.bfloat16)
    count_rows = utterances * frames
    act_rows = activated.reshape(count_rows, features)
    grad_rows = (cotangent * live_mask.astype(jnp.bfloat16)).reshape(count_rows, features)
    whole = lax.all_gather(weight, "batch", axis=0, tiled=True)
    projected = jnp.dot(act_rows, whole, preferred_element_type=jnp.float32)
    act_grad = transposed(grad_rows, whole)
    projected = projected.astype(jnp.bfloat16).reshape(utterances, frames, features)
    grad_weight = lax.psum_scatter(
        row_product(act_rows, grad_rows), ("batch", "tm"), scatter_dimension=0, tiled=True
    )
    act_grad = act_grad.reshape(utterances, frames, features)
    gain_grad, conv_grad = norm_backward(act_grad, scaled, normed, inv_scale, norm_gain, live_mask)
    kernel_grad = jnp.stack(
        [jnp.sum(conv_grad * padded[:, tap : tap + frames, :], axis=(0, 1)) for tap in range(taps)]
    )
    kernel_grad, gain_grad = lax.psum((kernel_grad, gain_grad), ("batch", "tm"))
    grad_pad = padded_2(conv_grad, (("tm", 1),), reach)
    back = jnp.zeros((utterances, frames, features), jnp.float32)
    for tap in range(taps):
        back = back + kernel[tap] * grad_pad[:, 2 * reach - tap : 2 * reach - tap + frames, :]
    grad_input = (back * live_mask).astype(jnp.bfloat16)
    return (projected, grad_input, grad_weight, kernel_grad, gain_grad)


def solution(mesh):
    in_specs = (
        P("batch", "tm", None),
        P("batch"),
        P(),
        P(),
        P("batch", None),
        P("batch", "tm", None),
    )
    out_specs = (P("batch", "tm", None), P("batch", "tm", None), P(("batch", "tm"), None), P(), P())
    return jax.shard_map(
        on_device, mesh=mesh, in_specs=in_specs, out_specs=out_specs, check_vma=False
    )
```

profile of v0, /device:TPU:1, one launch (start us, length us, event | category | flops | bytes accessed | tf_op | source)
XLA Modules:
  0.0 1614.6 jit_solution(4095045704864979232)
XLA Ops:
  31.8 718.6 %fusion = f32[8,1536]{1,0:T(8,128)S(1)} fusion(f32[1536,1536]{1,0:T(8,128)} %fusion.94), kind=kCustom, calls=%all-reduce-scatter | all-reduce-scatter fusion | flops 3145729 | bytes 9486336
  772.6 30.2 %collective-permute-start.51 = (f32[8,1536]{1,0:T(8,128)S(1)}, f32[8,1536]{1,0:T(8,128)S(1)}, u32[]{:S(2)}, u32[]{:S(2)}) collective-permute-start(f32[8,1536]{1,0:T(8,128)S(1)} %fusion), channel_id=1, source_target_pairs={{0,48},{1,49},{2,50},{3,51},{4,52},{5,53},{6,54},{7,55},{8,56},{9,... | collective-permute-start | bytes 147464
  851.6 13.1 collective-permute-start.33
  864.7 13.1 collective-permute-start.32
  877.9 13.1 collective-permute-start.31
  891.0 13.1 collective-permute-start.30
  904.2 13.1 collective-permute-start.29
  917.3 13.1 collective-permute-start.28
  930.5 13.1 collective-permute-start.27
  943.6 13.1 collective-permute-start.26
  956.8 13.1 collective-permute-start.25
  969.9 13.1 collective-permute-start.24
  983.1 13.1 collective-permute-start.23
  996.2 13.1 collective-permute-start.22
  1009.4 13.1 collective-permute-start.21
  1022.5 13.1 collective-permute-start.20
  1035.7 13.1 collective-permute-start.19
  1048.8 13.1 collective-permute-start.18
  1062.0 13.1 collective-permute-start.17
  1075.1 13.1 collective-permute-start.16
  1088.3 13.1 collective-permute-start.15
  1101.4 13.1 collective-permute-start.14
  1114.6 13.1 collective-permute-start.13
  1127.7 13.1 collective-permute-start.12
  1140.9 13.1 collective-permute-start.11
  1180.3 13.7 collective-permute-start.8
  1194.1 13.1 collective-permute-start.7
  1207.2 13.2 collective-permute-start.6
  1220.4 13.1 collective-permute-start.5
  1248.9 97.2 %concatenate.49 = f32[518,1536]{1,0:T(8,128)} concatenate(f32[6,1536]{1,0:T(8,128)S(1)} %collective-permute-done.67, f32[8,1536]{1,0:T(8,128)S(1)} %collective-permute-done.66, f32[8,1536]{1,0:T(8,128)S(1)} %collective-permute-done.65, f32[8,1536]{1,0:T(8,128)S(1)} %collective-permute-done.64, f32[8,1536]{1,0:T(8,128)S(1)} %collective-permute-done.63, ...), dimensions={0} | concatenate | bytes 6365184
  1368.4 81.5 %psum.15 = f32[1536]{0:T(1024)} all-reduce(f32[1536]{0:T(1024)S(1)} %get-tuple-element.36), channel_id=1, replica_groups=mesh['batch'=8,'tm'=32] {'batch','tm'}, use_global_device_ids=true, to_apply=%region_38.0 | all-reduce | flops 1536 | bytes 12288 | tf_op jit(solution)/shard_map/psum | solution.py:89
  1454.2 151.9 %all-reduce.4.cloned.1.call-done = f32[31,1536]{1,0:T(8,128)} async-done(((f32[31,1536]{1,0:T(8,128)}), f32[31,1536]{1,0:T(8,128)}) %all-reduce.4.cloned.1.call-update) | async-done | bytes 190480 | tf_op jit(solution)/shard_map/psum | solution.py:89
  (258 shorter events, 163.6 us)
Async XLA Ops:
  7.2 1340.5 %all-gather.2.cloned.1.call-start = ((), (), s32[]{:S(2)}) async-start(), calls=%async_computation | async-start | bytes 5308416 | tf_op jit(solution)/shard_map/all_gather | solution.py:77
  7.9 1598.2 %all-reduce.4.cloned.1.call-start = ((), (), s32[]{:S(2)}) async-start(), calls=%async_computation.1 | async-start | bytes 393216 | tf_op jit(solution)/shard_map/psum | solution.py:89
  845.4 58.8 %collective-permute-start.34 = (f32[8,1536]{1,0:T(8,128)S(1)}, f32[8,1536]{1,0:T(8,128)S(1)}, u32[]{:S(2)}, u32[]{:S(2)}) collective-permute-start(f32[8,1536]{1,0:T(8,128)S(1)} %fusion), channel_id=1, source_target_pairs={{0,31},{1,32},{2,33},{3,34},{4,35},{5,36},{6,37},{7,38},{8,39},{9,... | collective-permute-start | bytes 147464
  851.6 65.7 %collective-permute-start.33 = (f32[8,1536]{1,0:T(8,128)S(1)}, f32[8,1536]{1,0:T(8,128)S(1)}, u32[]{:S(2)}, u32[]{:S(2)}) collective-permute-start(f32[8,1536]{1,0:T(8,128)S(1)} %fusion), channel_id=1, source_target_pairs={{0,30},{1,31},{2,32},{3,33},{4,34},{5,35},{6,36},{7,37},{8,38},{9,... | collective-permute-start | bytes 147464
  864.7 65.7 %collective-permute-start.32 = (f32[8,1536]{1,0:T(8,128)S(1)}, f32[8,1536]{1,0:T(8,128)S(1)}, u32[]{:S(2)}, u32[]{:S(2)}) collective-permute-start(f32[8,1536]{1,0:T(8,128)S(1)} %fusion), channel_id=1, source_target_pairs={{0,29},{1,30},{2,31},{3,32},{4,33},{5,34},{6,35},{7,36},{8,37},{9,... | collective-permute-start | bytes 147464
  877.9 65.7 %collective-permute-start.31 = (f32[8,1536]{1,0:T(8,128)S(1)}, f32[8,1536]{1,0:T(8,128)S(1)}, u32[]{:S(2)}, u32[]{:S(2)}) collective-permute-start(f32[8,1536]{1,0:T(8,128)S(1)} %fusion), channel_id=1, source_target_pairs={{0,28},{1,29},{2,30},{3,31},{4,32},{5,33},{6,34},{7,35},{8,36},{9,... | collective-permute-start | bytes 147464
  891.0 65.7 %collective-permute-start.30 = (f32[8,1536]{1,0:T(8,128)S(1)}, f32[8,1536]{1,0:T(8,128)S(1)}, u32[]{:S(2)}, u32[]{:S(2)}) collective-permute-start(f32[8,1536]{1,0:T(8,128)S(1)} %fusion), channel_id=1, source_target_pairs={{0,27},{1,28},{2,29},{3,30},{4,31},{5,32},{6,33},{7,34},{8,35},{9,... | collective-permute-start | bytes 147464
  904.2 65.7 %collective-permute-start.29 = (f32[8,1536]{1,0:T(8,128)S(1)}, f32[8,1536]{1,0:T(8,128)S(1)}, u32[]{:S(2)}, u32[]{:S(2)}) collective-permute-start(f32[8,1536]{1,0:T(8,128)S(1)} %fusion), channel_id=1, source_target_pairs={{0,26},{1,27},{2,28},{3,29},{4,30},{5,31},{6,32},{7,33},{8,34},{9,... | collective-permute-start | bytes 147464
  917.3 65.7 %collective-permute-start.28 = (f32[8,1536]{1,0:T(8,128)S(1)}, f32[8,1536]{1,0:T(8,128)S(1)}, u32[]{:S(2)}, u32[]{:S(2)}) collective-permute-start(f32[8,1536]{1,0:T(8,128)S(1)} %fusion), channel_id=1, source_target_pairs={{0,25},{1,26},{2,27},{3,28},{4,29},{5,30},{6,31},{7,32},{8,33},{9,... | collective-permute-start | bytes 147464
  930.5 65.7 %collective-permute-start.27 = (f32[8,1536]{1,0:T(8,128)S(1)}, f32[8,1536]{1,0:T(8,128)S(1)}, u32[]{:S(2)}, u32[]{:S(2)}) collective-permute-start(f32[8,1536]{1,0:T(8,128)S(1)} %fusion), channel_id=1, source_target_pairs={{0,24},{1,25},{2,26},{3,27},{4,28},{5,29},{6,30},{7,31},{8,32},{9,... | collective-permute-start | bytes 147464
  943.6 65.7 %collective-permute-start.26 = (f32[8,1536]{1,0:T(8,128)S(1)}, f32[8,1536]{1,0:T(8,128)S(1)}, u32[]{:S(2)}, u32[]{:S(2)}) collective-permute-start(f32[8,1536]{1,0:T(8,128)S(1)} %fusion), channel_id=1, source_target_pairs={{0,23},{1,24},{2,25},{3,26},{4,27},{5,28},{6,29},{7,30},{8,31},{9,... | collective-permute-start | bytes 147464
  956.8 65.7 %collective-permute-start.25 = (f32[8,1536]{1,0:T(8,128)S(1)}, f32[8,1536]{1,0:T(8,128)S(1)}, u32[]{:S(2)}, u32[]{:S(2)}) collective-permute-start(f32[8,1536]{1,0:T(8,128)S(1)} %fusion), channel_id=1, source_target_pairs={{0,22},{1,23},{2,24},{3,25},{4,26},{5,27},{6,28},{7,29},{8,30},{9,... | collective-permute-start | bytes 147464
  969.9 65.7 %collective-permute-start.24 = (f32[8,1536]{1,0:T(8,128)S(1)}, f32[8,1536]{1,0:T(8,128)S(1)}, u32[]{:S(2)}, u32[]{:S(2)}) collective-permute-start(f32[8,1536]{1,0:T(8,128)S(1)} %fusion), channel_id=1, source_target_pairs={{0,21},{1,22},{2,23},{3,24},{4,25},{5,26},{6,27},{7,28},{8,29},{9,... | collective-permute-start | bytes 147464
  983.1 65.7 %collective-permute-start.23 = (f32[8,1536]{1,0:T(8,128)S(1)}, f32[8,1536]{1,0:T(8,128)S(1)}, u32[]{:S(2)}, u32[]{:S(2)}) collective-permute-start(f32[8,1536]{1,0:T(8,128)S(1)} %fusion), channel_id=1, source_target_pairs={{0,20},{1,21},{2,22},{3,23},{4,24},{5,25},{6,26},{7,27},{8,28},{9,... | collective-permute-start | bytes 147464
  996.2 65.7 %collective-permute-start.22 = (f32[8,1536]{1,0:T(8,128)S(1)}, f32[8,1536]{1,0:T(8,128)S(1)}, u32[]{:S(2)}, u32[]{:S(2)}) collective-permute-start(f32[8,1536]{1,0:T(8,128)S(1)} %fusion), channel_id=1, source_target_pairs={{0,19},{1,20},{2,21},{3,22},{4,23},{5,24},{6,25},{7,26},{8,27},{9,... | collective-permute-start | bytes 147464
  1009.4 65.7 %collective-permute-start.21 = (f32[8,1536]{1,0:T(8,128)S(1)}, f32[8,1536]{1,0:T(8,128)S(1)}, u32[]{:S(2)}, u32[]{:S(2)}) collective-permute-start(f32[8,1536]{1,0:T(8,128)S(1)} %fusion), channel_id=1, source_target_pairs={{0,18},{1,19},{2,20},{3,21},{4,22},{5,23},{6,24},{7,25},{8,26},{9,... | collective-permute-start | bytes 147464
  1022.5 65.7 %collective-permute-start.20 = (f32[8,1536]{1,0:T(8,128)S(1)}, f32[8,1536]{1,0:T(8,128)S(1)}, u32[]{:S(2)}, u32[]{:S(2)}) collective-permute-start(f32[8,1536]{1,0:T(8,128)S(1)} %fusion), channel_id=1, source_target_pairs={{0,17},{1,18},{2,19},{3,20},{4,21},{5,22},{6,23},{7,24},{8,25},{9,... | collective-permute-start | bytes 147464
  1035.7 65.7 %collective-permute-start.19 = (f32[8,1536]{1,0:T(8,128)S(1)}, f32[8,1536]{1,0:T(8,128)S(1)}, u32[]{:S(2)}, u32[]{:S(2)}) collective-permute-start(f32[8,1536]{1,0:T(8,128)S(1)} %fusion), channel_id=1, source_target_pairs={{0,16},{1,17},{2,18},{3,19},{4,20},{5,21},{6,22},{7,23},{8,24},{9,... | collective-permute-start | bytes 147464
  1048.8 65.7 %collective-permute-start.18 = (f32[8,1536]{1,0:T(8,128)S(1)}, f32[8,1536]{1,0:T(8,128)S(1)}, u32[]{:S(2)}, u32[]{:S(2)}) collective-permute-start(f32[8,1536]{1,0:T(8,128)S(1)} %fusion), channel_id=1, source_target_pairs={{0,15},{1,16},{2,17},{3,18},{4,19},{5,20},{6,21},{7,22},{8,23},{9,... | collective-permute-start | bytes 147464
  1062.0 65.7 %collective-permute-start.17 = (f32[8,1536]{1,0:T(8,128)S(1)}, f32[8,1536]{1,0:T(8,128)S(1)}, u32[]{:S(2)}, u32[]{:S(2)}) collective-permute-start(f32[8,1536]{1,0:T(8,128)S(1)} %fusion), channel_id=1, source_target_pairs={{0,14},{1,15},{2,16},{3,17},{4,18},{5,19},{6,20},{7,21},{8,22},{9,... | collective-permute-start | bytes 147464
  1075.1 65.7 %collective-permute-start.16 = (f32[8,1536]{1,0:T(8,128)S(1)}, f32[8,1536]{1,0:T(8,128)S(1)}, u32[]{:S(2)}, u32[]{:S(2)}) collective-permute-start(f32[8,1536]{1,0:T(8,128)S(1)} %fusion), channel_id=1, source_target_pairs={{0,13},{1,14},{2,15},{3,16},{4,17},{5,18},{6,19},{7,20},{8,21},{9,... | collective-permute-start | bytes 147464
  1088.3 65.7 %collective-permute-start.15 = (f32[8,1536]{1,0:T(8,128)S(1)}, f32[8,1536]{1,0:T(8,128)S(1)}, u32[]{:S(2)}, u32[]{:S(2)}) collective-permute-start(f32[8,1536]{1,0:T(8,128)S(1)} %fusion), channel_id=1, source_target_pairs={{0,12},{1,13},{2,14},{3,15},{4,16},{5,17},{6,18},{7,19},{8,20},{9,... | collective-permute-start | bytes 147464
  1101.4 65.7 %collective-permute-start.14 = (f32[8,1536]{1,0:T(8,128)S(1)}, f32[8,1536]{1,0:T(8,128)S(1)}, u32[]{:S(2)}, u32[]{:S(2)}) collective-permute-start(f32[8,1536]{1,0:T(8,128)S(1)} %fusion), channel_id=1, source_target_pairs={{0,11},{1,12},{2,13},{3,14},{4,15},{5,16},{6,17},{7,18},{8,19},{9,... | collective-permute-start | bytes 147464
  1114.6 65.7 %collective-permute-start.13 = (f32[8,1536]{1,0:T(8,128)S(1)}, f32[8,1536]{1,0:T(8,128)S(1)}, u32[]{:S(2)}, u32[]{:S(2)}) collective-permute-start(f32[8,1536]{1,0:T(8,128)S(1)} %fusion), channel_id=1, source_target_pairs={{0,10},{1,11},{2,12},{3,13},{4,14},{5,15},{6,16},{7,17},{8,18},{9,... | collective-permute-start | bytes 147464
  1127.7 66.3 %collective-permute-start.12 = (f32[8,1536]{1,0:T(8,128)S(1)}, f32[8,1536]{1,0:T(8,128)S(1)}, u32[]{:S(2)}, u32[]{:S(2)}) collective-permute-start(f32[8,1536]{1,0:T(8,128)S(1)} %fusion), channel_id=1, source_target_pairs={{0,9},{1,10},{2,11},{3,12},{4,13},{5,14},{6,15},{7,16},{8,17},{9,1... | collective-permute-start | bytes 147464
  1140.9 66.3 %collective-permute-start.11 = (f32[8,1536]{1,0:T(8,128)S(1)}, f32[8,1536]{1,0:T(8,128)S(1)}, u32[]{:S(2)}, u32[]{:S(2)}) collective-permute-start(f32[8,1536]{1,0:T(8,128)S(1)} %fusion), channel_id=1, source_target_pairs={{0,8},{1,9},{2,10},{3,11},{4,12},{5,13},{6,14},{7,15},{8,16},{9,17... | collective-permute-start | bytes 147464
  1154.0 66.3 %collective-permute-start.10 = (f32[8,1536]{1,0:T(8,128)S(1)}, f32[8,1536]{1,0:T(8,128)S(1)}, u32[]{:S(2)}, u32[]{:S(2)}) collective-permute-start(f32[8,1536]{1,0:T(8,128)S(1)} %fusion), channel_id=1, source_target_pairs={{0,7},{1,8},{2,9},{3,10},{4,11},{5,12},{6,13},{7,14},{8,15},{9,16}... | collective-permute-start | bytes 147464
  1167.2 66.3 %collective-permute-start.9 = (f32[8,1536]{1,0:T(8,128)S(1)}, f32[8,1536]{1,0:T(8,128)S(1)}, u32[]{:S(2)}, u32[]{:S(2)}) collective-permute-start(f32[8,1536]{1,0:T(8,128)S(1)} %fusion), channel_id=1, source_target_pairs={{0,6},{1,7},{2,8},{3,9},{4,10},{5,11},{6,12},{7,13},{8,14},{9,15},... | collective-permute-start | bytes 147464
  1180.3 66.3 %collective-permute-start.8 = (f32[8,1536]{1,0:T(8,128)S(1)}, f32[8,1536]{1,0:T(8,128)}, u32[]{:S(2)}, u32[]{:S(2)}) collective-permute-start(f32[8,1536]{1,0:T(8,128)S(1)} %fusion), channel_id=1, source_target_pairs={{0,5},{1,6},{2,7},{3,8},{4,9},{5,10},{6,11},{7,12},{8,13},{9,14},{... | collective-permute-start | bytes 147464
  1194.1 52.6 %collective-permute-start.7 = (f32[8,1536]{1,0:T(8,128)S(1)}, f32[8,1536]{1,0:T(8,128)}, u32[]{:S(2)}, u32[]{:S(2)}) collective-permute-start(f32[8,1536]{1,0:T(8,128)S(1)} %fusion), channel_id=1, source_target_pairs={{0,4},{1,5},{2,6},{3,7},{4,8},{5,9},{6,10},{7,11},{8,12},{9,13},{1... | collective-permute-start | bytes 147464
  1358.8 91.1 %collective-permute-start.2 = (f32[1,15,1536]{2,1,0:T(8,128)S(1)}, f32[1,15,1536]{2,1,0:T(8,128)S(1)}, u32[]{:S(2)}, u32[]{:S(2)}) collective-permute-start(f32[1,15,1536]{2,1,0:T(8,128)S(1)} %get-tuple-element.75), channel_id=1, source_target_pairs={{1,0},{2,1},{3,2},{4,3},{5,4},{6,5},{7,6},{8,7},{9,8},{10,9},{11,1... | collective-permute-start | bytes 276488 | tf_op jit(solution)/shard_map/ppermute | solution.py:17
  1360.9 89.0 %collective-permute-start.3 = (f32[1,15,1536]{2,1,0:T(8,128)S(1)}, f32[1,15,1536]{2,1,0:T(8,128)S(1)}, u32[]{:S(2)}, u32[]{:S(2)}) collective-permute-start(f32[1,15,1536]{2,1,0:T(8,128)S(1)} %get-tuple-element.76), channel_id=1, source_target_pairs={{0,1},{1,2},{2,3},{3,4},{4,5},{5,6},{6,7},{7,8},{8,9},{9,10},{10,1... | collective-permute-start | bytes 276488 | tf_op jit(solution)/shard_map/ppermute | solution.py:15
  (84 other events, 9688.6 us)
Sparse Core Ops, SparseCore 0:
  9.8 113.0 all-gather.1
  1358.9 247.1 all-reduce.3
where the time goes:
time: 1620 us; the launch traced here: 1610 us
  blocking collectives  800 us (49%)
  starting transfers between devices  506 us (31%)
  waiting for transfers between devices  156 us (10%)
  local copies, waits for them, and re-layouts  108 us (7%)
  between operations  16.6 us (1%)
    unnamed x1, blocking collectives  719 us
    unnamed x64, starting transfers between devices  493 us
    psum x1, waiting for transfers between devices, on_device(): kernel_grad, gain_grad = lax.psum((kernel_grad, gain_grad), ('batch', 'tm'))  152 us
    unnamed x96, local copies, waits for them, and re-layouts  101 us
    psum x1, blocking collectives, on_device(): kernel_grad, gain_grad = lax.psum((kernel_grad, gain_grad), ('batch', 'tm'))  81.5 us
  transfers between devices with their start and end apart: 70, of which 5 were waited for; matrix products, arithmetic and copies ran while one was open for 52% of the time, Pallas kernels for 0%

commit v1 on v0

v1 whole, which is shorter than its diff:
```python
import jax
import jax.numpy as jnp
from jax import lax
from jax.experimental import pallas as pl
from jax.experimental.pallas import tpu as pltpu
from jax.sharding import PartitionSpec as P

F32, BF16 = jnp.float32, jnp.bfloat16
MESH = pl.DeviceIdType.MESH
D, T, H, TAPS = 1536, 128, 768, 31
PAD = 16
LANES = 128
CHUNKS = D // LANES


def lanes_of(k):
    return pl.ds(pl.multiple_of(k * LANES, LANES), LANES)


def fused(
    x_ref, len_ref, kern_ref, gain_ref, w_ref, cot_ref,
    proj_ref, gin_ref, gw_ref, gk_ref, gg_ref,
    xm, hx, xf, cv, ds, ab, at, us, ub, wb, px, py, rx, ry, s2x, s2y, r2x, r2y,
    facc, zs, rz, fin, cr, agp, agr, pj, pjr, cg, gkb, gcr, gh, zr, xs, ys, fg, fgr,
    sem_halo_s, sem_halo_r, sem_w_s, sem_w_r, sem_c_s, sem_c_r, sem_p_s, sem_p_r,
    sem_z_s, sem_z_r, sem_t_s, sem_t_r,
):
    b = lax.axis_index("batch")
    t = lax.axis_index("tm")
    y, xl = b // 2, b % 2
    xh, z, c = t // 16, (t // 2) % 8, t % 2
    x = xh * 2 + xl
    oc = 1 - c

    def dev(y_, x_, z_, c_):
        return (y_ * 2 + x_ % 2, (x_ // 2) * 16 + z_ * 2 + c_)

    def along_y(i):
        return dev((y + i) % 4, x, z, c)

    def along_x(i):
        return dev(y, (x + i) % 4, z, c)

    def along_z(i):
        return dev(y, x, (z + i) % 8, c)

    mate = dev(y, x, z, oc)
    before, after = (b, t - 1), (b, t + 1)

    def block_of(x_):
        return (x_ % 2) * 2 + x_ // 2

    q = block_of(x)

    def half(c_):
        return pl.ds(pl.multiple_of(c_ * H, H), H)

    def frames_of(c_):
        return pl.ds(pl.multiple_of(c_ * T, T), T)

    started = []

    def copy(src, dst, ss, rs, to):
        return pltpu.make_async_remote_copy(
            src_ref=src, dst_ref=dst, send_sem=ss, recv_sem=rs, device_id=to, device_id_type=MESH
        )

    def send(*args):
        item = copy(*args)
        item.start()
        started.append(item)
        return item

    barrier = pltpu.get_barrier_semaphore()

    def greet(to):
        pl.semaphore_signal(barrier, inc=1, device_id=to, device_id_type=MESH)

    greet(mate)
    for i in range(1, 4):
        greet(along_y(i))
        greet(along_x(i))
    for i in range(1, 8):
        greet(along_z(i))

    @pl.when(t > 0)
    def _():
        greet(before)

    @pl.when(t < 31)
    def _():
        greet(after)

    length = len_ref[0]
    position = t * T + lax.broadcasted_iota(jnp.int32, (T, LANES), 0)
    live = jnp.where(position < length, 1.0, 0.0).astype(F32)

    def mask_chunk(k, _):
        at_lanes = lanes_of(k)
        masked = x_ref[:, at_lanes].astype(F32) * live
        xm[:, at_lanes] = masked.astype(BF16)
        xf[PAD:PAD + T, at_lanes] = masked
        us[:, at_lanes] = (cot_ref[:, at_lanes].astype(F32) * live).astype(BF16)
        return 0

    lax.fori_loop(0, CHUNKS, mask_chunk, 0)

    others = 14 + jnp.where(t > 0, 1, 0) + jnp.where(t < 31, 1, 0)
    pl.semaphore_wait(barrier, others)

    to_before = copy(xm.at[pl.ds(0, PAD)], hx.at[1], sem_halo_s.at[0], sem_halo_r.at[1], before)
    to_after = copy(xm.at[pl.ds(T - PAD, PAD)], hx.at[0], sem_halo_s.at[1], sem_halo_r.at[0], after)

    @pl.when(t > 0)
    def _():
        to_before.start()

    @pl.when(t < 31)
    def _():
        to_after.start()

    mine = w_ref.at[:, half(c)]

    def rows_of(y_, xl_, start, count):
        return pl.ds(pl.multiple_of((y_ * 2 + xl_) * 192 + start, 96), count)

    w_own = rows_of(y, xl, 0, 192)
    u_swap = send(us.at[:, half(oc)], ub.at[frames_of(c)], sem_c_s.at[0], sem_c_r.at[0], mate)
    for i in range(1, 4):
        send(mine, wb.at[w_own], sem_w_s.at[i - 1], sem_w_r.at[i - 1], along_y(i))
    for side, step in ((0, 1), (1, 3)):
        send(
            w_ref.at[pl.ds(side * 96, 96), half(c)], wb.at[rows_of(y, xl, side * 96, 96)],
            sem_w_s.at[3 + side], sem_w_r.at[3 + side], along_x(step),
        )
    wb[w_own, :] = w_ref[:, half(c)]
    ub[frames_of(c), :] = us[:, half(c)]

    @pl.when(t > 0)
    def _():
        to_after.wait_recv()
        xf[0:PAD, :] = hx[0].astype(F32)

    @pl.when(t == 0)
    def _():
        xf[0:PAD, :] = jnp.zeros((PAD, D), F32)

    @pl.when(t < 31)
    def _():
        to_before.wait_recv()
        xf[PAD + T:, :] = hx[1].astype(F32)

    @pl.when(t == 31)
    def _():
        xf[PAD + T:, :] = jnp.zeros((PAD, D), F32)

    def conv(source, taps, forward):
        total = jnp.zeros((T, LANES), F32)
        for r in range(8):
            shifted = source[r:r + T + 24]
            for k in range(4):
                offset = 8 * k + r
                tap = offset - 1 if forward else TAPS - offset
                if 0 <= tap < TAPS:
                    total = total + taps[tap:tap + 1] * shifted[8 * k:8 * k + T]
        return total

    def conv_chunk(k, total):
        at_lanes = lanes_of(k)
        value = conv(xf[:, at_lanes], kern_ref[:, at_lanes], True) * live
        cv[:, at_lanes] = value
        return total + value

    zero = jnp.zeros((T, LANES), F32)
    total = lax.fori_loop(0, CHUNKS, conv_chunk, zero)
    average = jnp.broadcast_to(jnp.sum(total, axis=1, keepdims=True) * (1.0 / D), (T, LANES))

    def variance_chunk(k, total):
        centred = cv[:, lanes_of(k)] - average
        return total + centred * centred

    total = lax.fori_loop(0, CHUNKS, variance_chunk, zero)
    variance = jnp.sum(total, axis=1, keepdims=True) * (1.0 / D)
    inv = jnp.broadcast_to(lax.rsqrt(variance + 1e-05), (T, LANES))

    def act_chunk(k, _):
        at_lanes = lanes_of(k)
        normed = (cv[:, at_lanes] - average) * inv
        scaled = normed * gain_ref[:, at_lanes]
        gate = 1.0 / (1.0 + jnp.exp(-scaled))
        act = scaled * gate
        cv[:, at_lanes] = normed
        ds[:, at_lanes] = gate * (1.0 + scaled * (1.0 - gate))
        ab[frames_of(c), at_lanes] = act.astype(BF16)
        at[lanes_of(k), frames_of(c)] = act.T.astype(BF16)
        return 0

    swaps = []
    for part in range(3):
        lax.fori_loop(part * 4, part * 4 + 4, act_chunk, 0)
        cols = pl.ds(part * 512, 512)
        here = at.at[cols, frames_of(c)]
        swaps.append(send(here, here, sem_c_s.at[1 + part], sem_c_r.at[1 + part], mate))
        here = ab.at[frames_of(c), cols]
        swaps.append(send(here, here, sem_c_s.at[4 + part], sem_c_r.at[4 + part], mate))

    for i in range(1, 4):
        from_y = (y + 4 - i) % 4
        copy(mine, wb.at[rows_of(from_y, xl, 0, 192)], sem_w_s.at[i - 1], sem_w_r.at[i - 1], along_y(i)).wait_recv()
        for side, step in ((0, 1), (1, 3)):
            here = wb.at[rows_of(from_y, xl, side * 96, 96)]
            n = 3 + 2 * i + side
            send(here, here, sem_w_s.at[n], sem_w_r.at[n], along_x(step))

    u_swap.wait_recv()
    for item in swaps[0::2]:
        item.wait_recv()

    def partial(dst, start):
        def body(n, _):
            rows = pl.ds(pl.multiple_of(n * 384, 384), 384)
            value = jnp.dot(at[rows, :], ub[:, start:start + 384], preferred_element_type=F32)
            dst[n] = value.reshape(4, 96, 384).astype(BF16)
            return 0
        lax.fori_loop(0, 4, body, 0)

    partial(px, 0)
    x_first = [
        send(px.at[:, block_of((x + i) % 4)], rx.at[i - 1], sem_p_s.at[i - 1], sem_p_r.at[i - 1], along_x(i))
        for i in range(1, 4)
    ]
    partial(py, 384)
    y_first = [
        send(py.at[(y + i) % 4], ry.at[i - 1], sem_p_s.at[2 + i], sem_p_r.at[2 + i], along_y(i))
        for i in range(1, 4)
    ]

    for i in range(4):
        from_y = (y + 4 - i) % 4
        for side, step in ((0, 1), (1, 3)):
            here = wb.at[rows_of(from_y, 1 - xl, side * 96, 96)]
            n = 3 + 2 * i + side
            copy(here, here, sem_w_s.at[n], sem_w_r.at[n], along_x(step)).wait_recv()

    def act_grad_chunk(n, _):
        cols = pl.ds(pl.multiple_of(n * 256, 256), 256)
        value = lax.dot_general(
            ub[...], wb[cols, :], (((1,), (1,)), ((), ())), preferred_element_type=F32
        )
        agp[0, :, cols] = value[:T]
        agp[1, :, cols] = value[T:]
        return 0

    ag_swaps = []
    for part in range(3):
        lax.fori_loop(part * 2, part * 2 + 2, act_grad_chunk, 0)
        cols = pl.ds(part * 512, 512)
        ag_swaps.append(
            send(agp.at[oc, :, cols], agr.at[:, cols], sem_c_s.at[7 + part], sem_c_r.at[7 + part], mate)
        )

    for item in swaps[1::2]:
        item.wait_recv()

    def project_chunk(n, _):
        cols = pl.ds(pl.multiple_of(n * 256, 256), 256)
        value = jnp.dot(ab[...], wb[:, cols], preferred_element_type=F32).astype(BF16)
        pj[0, :, cols] = value[:T]
        pj[1, :, cols] = value[T:]
        return 0

    lax.fori_loop(0, 3, project_chunk, 0)
    pj_swap = send(pj.at[oc], pjr, sem_c_s.at[10], sem_c_r.at[10], mate)
    proj_ref[:, half(c)] = pj[c]

    for item in ag_swaps:
        item.wait_recv()

    def back_chunk(k, sums):
        at_lanes = lanes_of(k)
        normed = cv[:, at_lanes]
        scaled_grad = (agp[c, :, at_lanes] + agr[:, at_lanes]) * ds[:, at_lanes]
        gkb[TAPS:TAPS + 1, at_lanes] = jnp.sum(scaled_grad * normed, axis=0, keepdims=True)
        normed_grad = scaled_grad * gain_ref[:, at_lanes]
        ds[:, at_lanes] = normed_grad
        return (sums[0] + normed_grad, sums[1] + normed_grad * normed)

    sums = lax.fori_loop(0, CHUNKS, back_chunk, (zero, zero))
    first, second = [
        jnp.broadcast_to(jnp.sum(s, axis=1, keepdims=True) * (1.0 / D), (T, LANES)) for s in sums
    ]
    inv_live = inv * live

    def conv_grad_chunk(k, _):
        at_lanes = lanes_of(k)
        cg[PAD:PAD + T, at_lanes] = inv_live * (ds[:, at_lanes] - first - cv[:, at_lanes] * second)
        return 0

    lax.fori_loop(0, CHUNKS, conv_grad_chunk, 0)

    g_before = copy(cg.at[pl.ds(PAD, PAD)], cg.at[pl.ds(PAD + T, PAD)], sem_halo_s.at[2], sem_halo_r.at[3], before)
    g_after = copy(cg.at[pl.ds(T, PAD)], cg.at[pl.ds(0, PAD)], sem_halo_s.at[3], sem_halo_r.at[2], after)

    @pl.when(t > 0)
    def _():
        g_before.start()

    @pl.when(t < 31)
    def _():
        g_after.start()

    def taps_chunk(k, _):
        at_lanes = lanes_of(k)
        source = xf[:, at_lanes]
        grad = cg[PAD:PAD + T, at_lanes]
        for r in range(8):
            shifted = source[r:r + T + 24]
            for j in range(4):
                tap = 8 * j + r - 1
                if 0 <= tap < TAPS:
                    gkb[tap:tap + 1, at_lanes] = jnp.sum(grad * shifted[8 * j:8 * j + T], axis=0, keepdims=True)
        return 0

    lax.fori_loop(0, CHUNKS, taps_chunk, 0)
    gk_swap = send(gkb.at[:, half(oc)], gcr, sem_t_s.at[0], sem_t_r.at[0], mate)

    for item in x_first:
        item.wait_recv()

    def add_x(n, _):
        value = px[n, q].astype(F32)
        for i in range(3):
            value = value + rx[i, n].astype(F32)
        s2x[n] = value.astype(BF16)
        return 0

    lax.fori_loop(0, 4, add_x, 0)
    x_second = [
        send(s2x.at[(y + i) % 4], r2x.at[i - 1], sem_p_s.at[5 + i], sem_p_r.at[5 + i], along_y(i))
        for i in range(1, 4)
    ]
    for item in y_first:
        item.wait_recv()

    def add_y(n, _):
        value = py[y, n].astype(F32)
        for i in range(3):
            value = value + ry[i, n].astype(F32)
        s2y[n] = value.astype(BF16)
        return 0

    lax.fori_loop(0, 4, add_y, 0)
    y_second = [
        send(s2y.at[block_of((x + i) % 4)], r2y.at[i - 1], sem_p_s.at[8 + i], sem_p_r.at[8 + i], along_x(i))
        for i in range(1, 4)
    ]

    def piece(z_):
        return (
            pl.ds(pl.multiple_of((z_ // 2) * 8, 8), 8),
            pl.ds(pl.multiple_of((z_ % 2) * 384, 384), 384),
        )

    gk_swap.wait_recv()
    gh[...] = gkb[:, half(c)] + gcr[...]
    t_z = [
        send(gh.at[piece((z + i) % 8)], zr.at[i - 1], sem_t_s.at[i], sem_t_r.at[i], along_z(i))
        for i in range(1, 8)
    ]

    @pl.when(t > 0)
    def _():
        g_after.wait_recv()

    @pl.when(t == 0)
    def _():
        cg[0:PAD, :] = jnp.zeros((PAD, D), F32)

    @pl.when(t < 31)
    def _():
        g_before.wait_recv()

    @pl.when(t == 31)
    def _():
        cg[PAD + T:, :] = jnp.zeros((PAD, D), F32)

    def input_chunk(k, _):
        at_lanes = lanes_of(k)
        value = conv(cg[:, at_lanes], kern_ref[:, at_lanes], False) * live
        gin_ref[:, at_lanes] = value.astype(BF16)
        return 0

    lax.fori_loop(0, 6, input_chunk, 0)

    for item in t_z:
        item.wait_recv()
    mine_t = gh[piece(z)]
    for i in range(7):
        mine_t = mine_t + zr[i]
    xs[x] = mine_t
    t_x = [send(xs.at[x], xs.at[x], sem_t_s.at[7 + i], sem_t_r.at[7 + i], along_x(i)) for i in range(1, 4)]

    for item in x_second + y_second:
        item.wait_recv()
    left, right = s2x[y].astype(F32), s2y[q].astype(F32)
    for i in range(3):
        left = left + r2x[i].astype(F32)
        right = right + r2y[i].astype(F32)
    facc[0:96, 0:384] = left
    facc[0:96, 384:768] = right
    facc[96:104, :] = jnp.zeros((8, H), F32)
    for n in range(8):
        zs[n] = facc[12 * n:12 * n + 16, :].astype(BF16)
    w_z = [
        send(zs.at[(z + i) % 8], rz.at[i - 1], sem_z_s.at[i - 1], sem_z_r.at[i - 1], along_z(i))
        for i in range(1, 8)
    ]

    def wait_slots(slots, me, sems, base):
        for i in range(1, 4):
            slot = slots.at[(me + 4 - i) % 4]
            copy(slot, slot, sem_t_s.at[base + i], sem_t_r.at[base + i], mate).wait_recv()

    wait_slots(xs, x, sem_t_r, 7)
    ys[y] = xs[0] + xs[1] + xs[2] + xs[3]
    t_y = [send(ys.at[y], ys.at[y], sem_t_s.at[10 + i], sem_t_r.at[10 + i], along_y(i)) for i in range(1, 4)]
    lax.fori_loop(6, CHUNKS, input_chunk, 0)
    wait_slots(ys, y, sem_t_r, 10)
    fg[piece(z)] = ys[0] + ys[1] + ys[2] + ys[3]
    for i in range(1, 8):
        here = fg.at[piece(z)]
        send(here, here, sem_t_s.at[13 + i], sem_t_r.at[13 + i], along_z(i))

    pj_swap.wait_recv()
    proj_ref[:, half(oc)] = pjr[...]

    for item in w_z:
        item.wait_recv()
    rows = zs[z].astype(F32)
    for i in range(7):
        rows = rows + rz[i].astype(F32)
    fin[...] = jnp.zeros((2, 8, H), F32)
    fin[0, 0:6, :] = rows[0:6]
    fin[1, 0:6, :] = rows[6:12]
    w_swap = send(fin.at[oc], cr, sem_z_s.at[7], sem_z_r.at[7], mate)

    for i in range(1, 8):
        slot = fg.at[piece((z + 8 - i) % 8)]
        copy(slot, slot, sem_t_s.at[13 + i], sem_t_r.at[13 + i], mate).wait_recv()
    t_swap = send(fg, fgr, sem_t_s.at[21], sem_t_r.at[21], mate)

    def put_taps(cols, value):
        gk_ref[:, cols] = value[0:TAPS]
        gg_ref[:, cols] = value[TAPS:TAPS + 1]

    put_taps(half(c), fg[...])
    gw_ref[:, half(c)] = fin[c][0:6]
    w_swap.wait_recv()
    gw_ref[:, half(oc)] = cr[0:6, :]
    t_swap.wait_recv()
    put_taps(half(oc), fgr[...])

    @pl.when(t > 0)
    def _():
        to_before.wait_send()
        g_before.wait_send()

    @pl.when(t < 31)
    def _():
        to_after.wait_send()
        g_after.wait_send()

    for item in started:
        item.wait_send()


def on_device(inputs, lengths, kernel, norm_gain, weight, cotangent):
    vmem = pl.BlockSpec(memory_space=pltpu.VMEM)
    dma = pltpu.SemaphoreType.DMA
    scratch = [
        pltpu.VMEM((T, D), BF16),
        pltpu.VMEM((2, PAD, D), BF16),
        pltpu.VMEM((T + 2 * PAD, D), F32),
        pltpu.VMEM((T, D), F32),
        pltpu.VMEM((T, D), F32),
        pltpu.VMEM((2 * T, D), BF16),
        pltpu.VMEM((D, 2 * T), BF16),
        pltpu.VMEM((T, D), BF16),
        pltpu.VMEM((2 * T, H), BF16),
        pltpu.VMEM((D, H), BF16),
        pltpu.VMEM((4, 4, 96, 384), BF16),
        pltpu.VMEM((4, 4, 96, 384), BF16),
        pltpu.VMEM((3, 4, 96, 384), BF16),
        pltpu.VMEM((3, 4, 96, 384), BF16),
        pltpu.VMEM((4, 96, 384), BF16),
        pltpu.VMEM((4, 96, 384), BF16),
        pltpu.VMEM((3, 96, 384), BF16),
        pltpu.VMEM((3, 96, 384), BF16),
        pltpu.VMEM((104, H), F32),
        pltpu.VMEM((8, 16, H), BF16),
        pltpu.VMEM((7, 16, H), BF16),
        pltpu.VMEM((2, 8, H), F32),
        pltpu.VMEM((8, H), F32),
        pltpu.VMEM((2, T, D), F32),
        pltpu.VMEM((T, D), F32),
        pltpu.VMEM((2, T, H), BF16),
        pltpu.VMEM((T, H), BF16),
        pltpu.VMEM((T + 2 * PAD, D), F32),
        pltpu.VMEM((32, D), F32),
        pltpu.VMEM((32, H), F32),
        pltpu.VMEM((32, H), F32),
        pltpu.VMEM((7, 8, 384), F32),
        pltpu.VMEM((4, 8, 384), F32),
        pltpu.VMEM((4, 8, 384), F32),
        pltpu.VMEM((32, H), F32),
        pltpu.VMEM((32, H), F32),
        dma((4,)), dma((4,)),
        dma((11,)), dma((11,)),
        dma((11,)), dma((11,)),
        dma((12,)), dma((12,)),
        dma((8,)), dma((8,)),
        dma((22,)), dma((22,)),
    ]
    projected, grad_input, grad_weight, grad_kernel, grad_gain = pl.pallas_call(
        fused,
        out_shape=(
            jax.ShapeDtypeStruct((T, D), BF16),
            jax.ShapeDtypeStruct((T, D), BF16),
            jax.ShapeDtypeStruct((6, D), F32),
            jax.ShapeDtypeStruct((TAPS, D), F32),
            jax.ShapeDtypeStruct((1, D), F32),
        ),
        in_specs=[vmem, pl.BlockSpec(memory_space=pltpu.SMEM), vmem, vmem, vmem, vmem],
        out_specs=[vmem] * 5,
        scratch_shapes=scratch,
        compiler_params=pltpu.CompilerParams(
            collective_id=0, has_side_effects=True, vmem_limit_bytes=48 << 20
        ),
        name="conv_module",
    )(inputs[0], lengths, kernel, norm_gain[None], weight, cotangent[0])
    return (projected[None], grad_input[None], grad_weight, grad_kernel, grad_gain[0])


def solution(mesh):
    in_specs = (
        P("batch", "tm", None),
        P("batch"),
        P(),
        P(),
        P("batch", None),
        P("batch", "tm", None),
    )
    out_specs = (P("batch", "tm", None), P("batch", "tm", None), P(("batch", "tm"), None), P(), P())
    return jax.shard_map(
        on_device, mesh=mesh, in_specs=in_specs, out_specs=out_specs, check_vma=False
    )
```

time: 1620 us -> 78.7 us (0.05)
  blocking collectives: 800 us -> 0 us
  starting transfers between devices: 506 us -> 0 us
  waiting for transfers between devices: 156 us -> 0 us
  local copies, waits for them, and re-layouts: 108 us -> 7.47 us
  Pallas kernels: 0 us -> 69 us
    unnamed x1 -> x0, blocking collectives: 719 us -> none
    unnamed x64 -> x0, starting transfers between devices: 493 us -> none
    psum x1 -> x0, waiting for transfers between devices: 152 us -> none  [on_device(): kernel_grad, gain_grad = lax.psum((kernel_grad, gain_grad), ('batch', 'tm'))]
    unnamed x96 -> x12, local copies, waits for them, and re-layouts: 101 us -> 6.77 us
    psum x1 -> x0, blocking collectives: 81.5 us -> none  [on_device(): kernel_grad, gain_grad = lax.psum((kernel_grad, gain_grad), ('batch', 'tm'))]
    pallas_call x0 -> x1, Pallas kernels: none -> 69 us  [on_device(): pl.pallas_call(fused, out_shape=(jax.ShapeDtypeStruct((T, D), BF16), jax....]
  transfers between devices with their start and end apart: 70 -> 0, of which waited for: 5 -> 0; matrix products, arithmetic and copies ran while one was open for 52% -> 0% of each run, Pallas kernels for 0% -> 0%
where the time goes in v1:
time: 78.7 us; the launch traced here: 78.4 us
  Pallas kernels  69 us (88%)
  local copies, waits for them, and re-layouts  7.47 us (9%)
  between operations  1.29 us (2%)
    pallas_call x1, Pallas kernels, on_device(): pl.pallas_call(fused, out_shape=(jax.ShapeDtypeStruct((T, D), BF16), jax....  69 us
    unnamed x12, local copies, waits for them, and re-layouts  6.77 us

profile of v1, /device:TPU:1, one launch (start us, length us, event | category | flops | bytes accessed | tf_op | source)
XLA Modules:
  0.0 78.4 jit_solution(12394821285402309910)
XLA Ops:
  1.3 0.7 broadcast_in_dim.9.gain_ref
  2.0 0.0 copy-start
  2.0 1.1 %copy-done = bf16[192,1536]{1,0:T(8,128)(2,1)S(1)} copy-done((bf16[192,1536]{1,0:T(8,128)(2,1)S(1)}, bf16[192,1536]{1,0:T(8,128)(2,1)}, u32[]{:S(2)}) %copy-start) | copy-done | bytes 589848
  3.0 0.0 copy-start.1
  3.0 1.0 %copy-done.1 = bf16[1,128,1536]{2,1,0:T(8,128)(2,1)S(1)} copy-done((bf16[1,128,1536]{2,1,0:T(8,128)(2,1)S(1)}, bf16[1,128,1536]{2,1,0:T(8,128)(2,1)}, u32[]{:S(2)}) %copy-start.1) | copy-done | bytes 393240
  4.0 0.0 copy-start.2
  4.0 1.0 %copy-done.2 = bf16[1,128,1536]{2,1,0:T(8,128)(2,1)S(1)} copy-done((bf16[1,128,1536]{2,1,0:T(8,128)(2,1)S(1)}, bf16[1,128,1536]{2,1,0:T(8,128)(2,1)}, u32[]{:S(2)}) %copy-start.2) | copy-done | bytes 393240
  5.0 0.0 copy-start.3
  5.0 0.9 %copy-done.3 = f32[31,1536]{1,0:T(8,128)S(1)} copy-done((f32[31,1536]{1,0:T(8,128)S(1)}, f32[31,1536]{1,0:T(8,128)}, u32[]{:S(2)}) %copy-start.3) | copy-done | bytes 190488
  6.0 69.0 %conv_module.1 = (bf16[128,1536]{1,0:T(8,128)(2,1)S(1)}, bf16[128,1536]{1,0:T(8,128)(2,1)S(1)}, f32[6,1536]{1,0:T(8,128)S(1)}, f32[31,1536]{1,0:T(8,128)S(1)}, f32[1,1536]{1,0:T(1,128)S(1)}) custom-call(bf16[128,1536]{1,0:T(8,128)(2,1)S(1)} %bitcast.6, s32[1]{0:T(128)S(6)} %copy.15.len_ref, f32[31,1536]{1,0:T(8,128)S(1)} %copy-done.3, ...), custom_call_target="tpu_custom_call" | custom-call | tf_op jit(solution)/shard_map/conv_module/pallas_call | solution.py:524
  75.0 0.6 reduce
  75.6 0.7 copy.16
  76.4 0.7 copy.17
  77.1 0.6 copy.18
  77.7 0.7 copy.19
Async XLA Ops:
  2.0 1.1 %copy-start = (bf16[192,1536]{1,0:T(8,128)(2,1)S(1)}, bf16[192,1536]{1,0:T(8,128)(2,1)}, u32[]{:S(2)}) copy-start(bf16[192,1536]{1,0:T(8,128)(2,1)} %w_ref.1) | copy-start | bytes 1769476
  3.0 1.0 %copy-start.1 = (bf16[1,128,1536]{2,1,0:T(8,128)(2,1)S(1)}, bf16[1,128,1536]{2,1,0:T(8,128)(2,1)}, u32[]{:S(2)}) copy-start(bf16[1,128,1536]{2,1,0:T(8,128)(2,1)} %param.6) | copy-start | bytes 1179652
  4.0 1.0 %copy-start.2 = (bf16[1,128,1536]{2,1,0:T(8,128)(2,1)S(1)}, bf16[1,128,1536]{2,1,0:T(8,128)(2,1)}, u32[]{:S(2)}) copy-start(bf16[1,128,1536]{2,1,0:T(8,128)(2,1)} %param.11) | copy-start | bytes 1179652
  5.0 0.9 %copy-start.3 = (f32[31,1536]{1,0:T(8,128)S(1)}, f32[31,1536]{1,0:T(8,128)}, u32[]{:S(2)}) copy-start(f32[31,1536]{1,0:T(8,128)} %kern_ref.1) | copy-start | bytes 571396
